TPU v7x, 32 devices: a whole 2x2x4 slice. The times are simulated.
32 devices in a mesh: seq: 16 (over z, x, core), kvh: 2 (over y).
Axes of the slice: x: 2, y: 2, z: 4, core: 2. Of those that a mesh axis runs over, the one named last changes fastest.
Arguments:
- queries: bfloat16 [4096, 12288], P('seq', 'kvh'), may hold values from -4 to 4
- keys: bfloat16 [4096, 1024], P('seq', 'kvh'), may hold values from -10 to 10
- values: bfloat16 [4096, 1024], P('seq', 'kvh'), may hold values from -6 to 6
- answer_lengths: int32 [4], replicated, may hold values from 512 to 2048, as said below
Outputs:
- attended: bfloat16 [4096, 12288], P(('seq', 'kvh'))
Inputs may be any that keep to these rules, and one draw needn't show every extreme that they name: `answer_lengths`: every length is a multiple of 256; the lengths sum to 4096; exactly one answer has the largest length 2048, every other one at most (7) * 256.
All inputs are finite; a program needn't handle non-finite values.
Results may differ from a plain program's by a relative error of at most 0.0035.
Values may be sent and summed in bfloat16 or wider, within the bound.
No kernel may reach another device: no remote copies, remote signals or barrier semaphores. Data moves between devices by JAX's collectives and lax.ppermute only.
A program may use at most 64 MiB of HBM per device.

v0:
```python
import math

import jax
import jax.numpy as jnp
from jax import lax
from jax.experimental import pallas as pl
from jax.experimental.pallas import tpu as pltpu
from jax.sharding import PartitionSpec as P

QUERY_PER_KEY = 12
HEAD_WIDTH = 128
GROUP_WIDTH = QUERY_PER_KEY * HEAD_WIDTH
SCALE_LOG2 = math.log2(math.e) / math.sqrt(HEAD_WIDTH)
VMEM_LIMIT = 62 * 1024 * 1024
STACK = 4
STACKS = QUERY_PER_KEY // STACK


def lanes(start):
    return pl.ds(pl.multiple_of(start * HEAD_WIDTH, HEAD_WIDTH), HEAD_WIDTH)


def first_visible(meta, position):
    end = jnp.int32(0)
    start = jnp.int32(0)
    for answer in range(2, meta.shape[0]):
        end = end + meta[answer]
        start = jnp.where(end <= position, end, start)
    return start


def attend_rows(count, offset, q_ref, out_ref, work, block):
    rows = q_ref.shape[0]
    stacked = STACK * rows
    window, nearest, probs, stack, staged, facing = work[:6]
    width = count * block
    first = window.shape[0] - width
    tokens = lax.rem(lax.broadcasted_iota(jnp.int32, (stacked, block), 0), rows) + offset
    mask = lax.broadcasted_iota(jnp.int32, (stacked, block), 1) <= tokens

    def load(number):
        for h in range(STACK):
            stack[h * rows : (h + 1) * rows, :HEAD_WIDTH] = q_ref[:, lanes(number * STACK + h)]

    def score(slot):
        keys = window[first + slot * block : first + (slot + 1) * block, : 2 * HEAD_WIDTH]
        return lax.dot_general(
            stack[...], keys, (((1,), (1,)), ((), ())), preferred_element_type=jnp.float32
        )

    def begin():
        ones = window[first : first + HEAD_WIDTH, HEAD_WIDTH : 2 * HEAD_WIDTH]
        column = lax.broadcasted_iota(jnp.int32, (rows, HEAD_WIDTH), 1)
        for h in range(STACK):
            at = slice(h * rows, (h + 1) * rows)
            same = jnp.dot(
                stack[at, :HEAD_WIDTH] * facing[...], ones, preferred_element_type=jnp.float32
            )
            stack[at, HEAD_WIDTH:] = jnp.where(column == 0, -same, 0.0).astype(stack.dtype)
        nearest[...] = jnp.where(mask, score(count - 1), -1e30)

    def soften(found, slot):
        for piece in range(block // HEAD_WIDTH):
            at = slice(piece * HEAD_WIDTH, (piece + 1) * HEAD_WIDTH)
            weights = jnp.exp2(found[:, at] * SCALE_LOG2)
            start = slot * block + piece * HEAD_WIDTH
            probs[:, start : start + HEAD_WIDTH] = weights.astype(jnp.bfloat16)

    def weigh():
        ahead = score(0) if count > 1 else None
        soften(nearest, count - 1)
        for slot in range(count - 1):
            found = ahead
            if slot < count - 2:
                ahead = score(slot + 1)
            soften(found, slot)

    def blend():
        found = jnp.dot(
            probs[:, :width], window[first:, HEAD_WIDTH:], preferred_element_type=jnp.float32
        )
        total = found[:, :HEAD_WIDTH]
        guess = pl.reciprocal(total, approx=True)
        guess = guess * (2.0 - total * guess)
        staged[...] = (found[:, HEAD_WIDTH:] * guess).astype(staged.dtype)
        return total

    def release(number):
        for h in range(STACK):
            out_ref[:, lanes(number * STACK + h)] = staged[h * rows : (h + 1) * rows]

    load(0)
    begin()

    def step(number, most):
        weigh()
        load(jnp.minimum(number + 1, STACKS - 1))
        begin()
        total = blend()
        for row in range(0, stacked, 8):
            most = jnp.maximum(most, total[row : row + 8])
        release(number)
        return most

    return jnp.max(lax.fori_loop(0, STACKS, step, jnp.zeros((8, HEAD_WIDTH), jnp.float32)))


def attend_rows_wide(visible, offset, q_ref, out_ref, work, block):
    rows = q_ref.shape[0]
    window, (peak, total, blended) = work[0], work[6:9]
    last = window.shape[0] - block
    tokens = lax.broadcasted_iota(jnp.int32, (rows, block), 0) + offset
    columns = lax.broadcasted_iota(jnp.int32, (rows, block), 1)

    @pl.loop(0, QUERY_PER_KEY)
    def _(head):
        peak[...] = jnp.full(peak.shape, -1e30, jnp.float32)
        total[...] = jnp.zeros(total.shape, jnp.float32)
        blended[...] = jnp.zeros(blended.shape, jnp.float32)

        @pl.loop(0, visible)
        def _(back):
            at = pl.ds(pl.multiple_of(last - back * block, block), block)
            found = lax.dot_general(
                q_ref[:, lanes(head)],
                window[at, :HEAD_WIDTH],
                (((1,), (1,)), ((), ())),
                preferred_element_type=jnp.float32,
            )
            found = jnp.where(columns <= tokens + back * block, found * SCALE_LOG2, -1e30)
            before = peak[...]
            now = jnp.maximum(before, jnp.max(found, axis=-1, keepdims=True))
            weights = jnp.exp2(found - now[:, :1])
            shrink = jnp.exp2(before - now)
            peak[...] = now
            total[...] = total[...] * shrink + jnp.sum(weights, axis=-1, keepdims=True)
            blended[...] = blended[...] * shrink + jnp.dot(
                weights.astype(jnp.bfloat16),
                window[at, 2 * HEAD_WIDTH :],
                preferred_element_type=jnp.float32,
            )

        out_ref[:, lanes(head)] = (blended[...] / total[...]).astype(out_ref.dtype)


def buffers_for(rows, span, block):
    stacked = STACK * rows
    return [
        pltpu.VMEM((span * block, 3 * HEAD_WIDTH), jnp.bfloat16),
        pltpu.VMEM((stacked, block), jnp.float32),
        pltpu.VMEM((stacked, span * block), jnp.bfloat16),
        pltpu.VMEM((stacked, 2 * HEAD_WIDTH), jnp.bfloat16),
        pltpu.VMEM((stacked, HEAD_WIDTH), jnp.bfloat16),
        pltpu.VMEM((rows, HEAD_WIDTH), jnp.bfloat16),
        pltpu.VMEM((rows, HEAD_WIDTH), jnp.float32),
        pltpu.VMEM((rows, HEAD_WIDTH), jnp.float32),
        pltpu.VMEM((rows, HEAD_WIDTH), jnp.float32),
        pltpu.SMEM((1,), jnp.float32),
    ]


WORK = 10


def attend_jobs(jobs, position_of, q_jobs, out_jobs, arrived, origin, meta, work, block, span, done=None):
    work[0][:, HEAD_WIDTH : 2 * HEAD_WIDTH] = jnp.ones((span * block, HEAD_WIDTH), jnp.bfloat16)

    @pl.loop(0, jobs)
    def _(job):
        index, offset = position_of(job)
        start = lax.div(first_visible(meta, index * block), block)
        visible = index - start + 1
        last = (index - origin + 1 - span) * block
        window, facing, most = work[0], work[5], work[9]
        moved = pl.ds(pl.multiple_of(last, block), span * block)
        window[:, :HEAD_WIDTH] = arrived[moved, :HEAD_WIDTH]
        window[:, 2 * HEAD_WIDTH :] = arrived[moved, HEAD_WIDTH:]
        here = pl.ds(pl.multiple_of(last + (span - 1) * block + offset, facing.shape[0]), facing.shape[0])
        facing[...] = arrived[here, :HEAD_WIDTH]
        for count in range(1, span + 1):

            @pl.when(visible == count)
            def _():
                most[0] = attend_rows(count, offset, q_jobs.at[job], out_jobs.at[job], work, block)

        @pl.when(jnp.logical_not(most[0] < 2.0**120))
        def _():
            attend_rows_wide(visible, offset, q_jobs.at[job], out_jobs.at[job], work, block)

        if done is not None:
            done(job)


PARTS = (0, 1, 2, 3)


def place_columns(meta, source, which):
    core, group = lax.rem(meta[0], 2), meta[1]
    from_core = 1 - core if source % 2 else core
    from_group = 1 - group if source // 2 else group
    column = ((from_group * 2 + from_core) * 2 + which) * GROUP_WIDTH
    return pl.ds(pl.multiple_of(column, GROUP_WIDTH), GROUP_WIDTH)


def place_copies(meta, inputs, sources, which, out, held, sems):
    loads, stores = [], []
    for number, (source, ref) in enumerate(zip(sources, inputs)):
        at = place_columns(meta, source, which)
        loads.append(pltpu.make_async_copy(ref, held.at[number], sems.at[0, number]))
        stores.append(pltpu.make_async_copy(held.at[number], out.at[:, at], sems.at[1, number]))
    return loads, stores


def place_kernel(meta, *refs, which, sources):
    count = len(sources)
    out, held, sems = refs[-3:]
    loads, stores = place_copies(meta, refs[:count], sources, which, out, held, sems)
    for load in loads:
        load.start()
    for load, store in zip(loads, stores):
        load.wait()
        store.start()
    for store in stores:
        store.wait()


def place(meta, arrays, sources, which, out):
    rows, count = arrays[0].shape[0], len(arrays)
    return pl.pallas_call(
        lambda *refs: place_kernel(*refs, which=which, sources=sources),
        out_shape=jax.ShapeDtypeStruct(out.shape, out.dtype),
        grid_spec=pltpu.PrefetchScalarGridSpec(
            num_scalar_prefetch=1,
            grid=(),
            in_specs=[pl.BlockSpec(memory_space=pl.ANY)] * (count + 1),
            out_specs=pl.BlockSpec(memory_space=pltpu.HBM),
            scratch_shapes=[
                pltpu.VMEM((count, rows, GROUP_WIDTH), jnp.bfloat16),
                pltpu.SemaphoreType.DMA((2, count)),
            ],
        ),
        input_output_aliases={1 + count: 0},
        compiler_params=pltpu.CompilerParams(vmem_limit_bytes=8 * 1024 * 1024),
        cost_estimate=estimate(),
    )(meta, *arrays, out)


def pair_kernel(
    meta, queries, theirs, *refs, flip_half, which, jobs, block, span, pieces, placed
):
    window, q_jobs, out_jobs, sems, held, held_sems = refs[-6 - WORK : -WORK]
    outs = refs[-6 - WORK - jobs : -6 - WORK]
    work = refs[-WORK:]
    rows = q_jobs.shape[1]
    mine, group = meta[0], meta[1]
    core = lax.rem(mine, 2)
    right = lax.rem(lax.div(mine, 2), 2)
    origin = mine - core - (span - 1)

    def half_of(job):
        return 1 - group if flip_half and job < 2 else group


    def fill(source, source_row, slot, size, sem):
        return pltpu.make_async_copy(
            source.at[pl.ds(source_row, size)], window.at[pl.ds(slot * block, size)], sems.at[sem]
        )

    if pieces == 5:
        fixed = [fill(refs[4], 0, 0, block, 0)]
        for back in range(4):
            fixed.append(fill(refs[back], 0, 7 - 2 * back, 2 * block, back + 1))
        by_side = []
    else:
        own, near, far, side_own, side_near, side_far = refs[:6]
        fixed = [
            fill(far, block, 0, block, 0),
            fill(near, 0, 3, 2 * block, 1),
            fill(own, 0, 7, 2 * block, 2),
        ]
        by_side = [
            (fill(side_far, 0, 1, 2 * block, 3), fill(side_near, 0, 1, 2 * block, 3)),
            (fill(side_near, 0, 5, 2 * block, 4), fill(side_own, 0, 5, 2 * block, 4)),
        ]
    for job in range(jobs):
        source = queries if job % 2 else theirs
        at = pl.ds(pl.multiple_of((2 * core + which) * GROUP_WIDTH, GROUP_WIDTH), GROUP_WIDTH)
        fixed.append(
            pltpu.make_async_copy(
                source.at[pl.ds(pl.multiple_of(half_of(job) * rows, rows), rows), at],
                q_jobs.at[job],
                sems.at[5 + job],
            )
        )
    for copy in fixed:
        copy.start()
    for on_left, on_right in by_side:
        pl.when(right == 0)(on_left.start)
        pl.when(right == 1)(on_right.start)
    for copy in fixed:
        copy.wait()
    for on_left, _ in by_side:
        on_left.wait()

    def position_of(job):
        half = jnp.where(job < 2, half_of(0), half_of(2))
        return mine - core + jnp.where(lax.rem(job, 2) == 0, 1 - core, core), half * rows

    if placed:
        loads, stores = place_copies(
            meta, refs[pieces : pieces + placed], PARTS, 0, outs[-1], held, held_sems
        )
        for load in loads:
            load.start()
        targets = [*outs[:-1], outs[-1].at[:, place_columns(meta, 0, which)]]
    else:
        loads, stores = [], []
        targets = outs
    copies = [
        pltpu.make_async_copy(out_jobs.at[job], out, sems.at[5 + job])
        for job, out in enumerate(targets)
    ]

    def done(job):
        for number, copy in enumerate(copies):
            pl.when(job == number)(copy.start)

    attend_jobs(
        jobs, position_of, q_jobs, out_jobs, window, origin, meta, work, block, span, done
    )
    for load, store in zip(loads, stores):
        load.wait()
        store.start()
    for copy in [*stores, *copies]:
        copy.wait()


def estimate(long=True):
    flops = 8_000_000_000 if long else 400_000_000
    return pl.CostEstimate(flops=flops, bytes_accessed=400_000, transcendentals=0)


def attend_pair(
    meta, queries, theirs, pieces, placed, earlier, flip_half, which, jobs, rows, span
):
    block = queries.shape[0]
    args = [queries, theirs, *pieces, *placed, *earlier]
    widths = [GROUP_WIDTH] * (jobs - 1) + [8 * GROUP_WIDTH if placed else GROUP_WIDTH]
    return pl.pallas_call(
        lambda *refs: pair_kernel(
            *refs,
            flip_half=flip_half,
            which=which,
            jobs=jobs,
            block=block,
            span=span,
            pieces=len(pieces),
            placed=len(placed),
        ),
        out_shape=[jax.ShapeDtypeStruct((rows, width), jnp.bfloat16) for width in widths],
        grid_spec=pltpu.PrefetchScalarGridSpec(
            num_scalar_prefetch=1,
            grid=(),
            in_specs=[pl.BlockSpec(memory_space=pltpu.HBM)] * len(args),
            out_specs=[pl.BlockSpec(memory_space=pltpu.HBM)] * jobs,
            scratch_shapes=[
                pltpu.VMEM(((span + 1) * block, 2 * HEAD_WIDTH), jnp.bfloat16),
                pltpu.VMEM((jobs, rows, GROUP_WIDTH), jnp.bfloat16),
                pltpu.VMEM((jobs, rows, GROUP_WIDTH), jnp.bfloat16),
                pltpu.SemaphoreType.DMA((5 + jobs,)),
                pltpu.VMEM((max(len(placed), 1), rows, GROUP_WIDTH), jnp.bfloat16),
                pltpu.SemaphoreType.DMA((2, max(len(placed), 1))),
                *buffers_for(rows, span, block),
            ],
        ),
        compiler_params=pltpu.CompilerParams(vmem_limit_bytes=VMEM_LIMIT),
        cost_estimate=estimate(len(earlier) > 0),
    )(meta, *args)


def own_kernel(meta, keys, values, theirs, *refs):
    outs, items, sems = refs[:3], refs[3], refs[4]
    core = lax.rem(meta[0], 2)
    block = keys.shape[0]
    mine = pl.ds(pl.multiple_of(core * block, block), block)
    other = pl.ds(pl.multiple_of((1 - core) * block, block), block)
    loads = []
    for which in range(2):
        for part, source in enumerate((keys, values)):
            at = slice(part * HEAD_WIDTH, (part + 1) * HEAD_WIDTH)
            loads.append((source.at[:, lanes(2 * core + which)], items.at[which, mine, at]))
            from_them = slice((2 * part + which) * HEAD_WIDTH, (2 * part + which + 1) * HEAD_WIDTH)
            loads.append((theirs.at[:, from_them], items.at[which, other, at]))
    loads = [
        pltpu.make_async_copy(source, target, sems.at[number])
        for number, (source, target) in enumerate(loads)
    ]
    stores = [
        pltpu.make_async_copy(items.at[which], outs[which], sems.at[8 + which])
        for which in range(2)
    ]
    more = [
        pltpu.make_async_copy(items.at[1, pl.ds(block, block)], outs[2], sems.at[10]),
    ]
    for load in loads:
        load.start()
    for which in range(2):
        for load in loads[4 * which : 4 * which + 4]:
            load.wait()
        stores[which].start()
    for store in more:
        store.start()
    for store in [*stores, *more]:
        store.wait()


def own_items(meta, keys, values, their_kv):
    block = keys.shape[0]
    shape = (2 * block, 2 * HEAD_WIDTH)
    return pl.pallas_call(
        own_kernel,
        out_shape=[jax.ShapeDtypeStruct((n * block, shape[1]), jnp.bfloat16) for n in (2, 2, 1)],
        grid_spec=pltpu.PrefetchScalarGridSpec(
            num_scalar_prefetch=1,
            grid=(),
            in_specs=[pl.BlockSpec(memory_space=pltpu.HBM)] * 3,
            out_specs=[pl.BlockSpec(memory_space=pltpu.HBM)] * 3,
            scratch_shapes=[pltpu.VMEM((2, *shape), jnp.bfloat16), pltpu.SemaphoreType.DMA((11,))],
        ),
        compiler_params=pltpu.CompilerParams(vmem_limit_bytes=VMEM_LIMIT),
    )(meta, keys, values, their_kv)


def after(values, earlier):
    return pl.pallas_call(
        lambda *refs: None,
        out_shape=[jax.ShapeDtypeStruct(value.shape, value.dtype) for value in values],
        in_specs=[pl.BlockSpec(memory_space=pltpu.HBM)] * (len(values) + len(earlier)),
        out_specs=[pl.BlockSpec(memory_space=pltpu.HBM)] * len(values),
        input_output_aliases={n: n for n in range(len(values))},
    )(*values, *earlier)


def whole_kernel(meta, queries, gathered, out, window, q_jobs, out_jobs, sems, *work, which, block, span):
    jobs, rows = q_jobs.shape[0], q_jobs.shape[1]
    mine = meta[0]
    origin = mine - (span - 1)
    copies = []
    for slot in range(span):
        at = pl.ds(pl.multiple_of(jnp.maximum(origin + slot, 0) * block, block), block)
        copies.append(
            pltpu.make_async_copy(
                gathered.at[at], window.at[pl.ds(slot * block, block)], sems.at[jobs + slot]
            )
        )
    at = pl.ds(which * GROUP_WIDTH, GROUP_WIDTH)
    for job in range(jobs):
        copies.append(
            pltpu.make_async_copy(
                queries.at[pl.ds(job * rows, rows), at], q_jobs.at[job], sems.at[job]
            )
        )
    for copy in copies:
        copy.start()
    for copy in copies:
        copy.wait()
    attend_jobs(
        jobs,
        lambda job: (mine, job * rows),
        q_jobs,
        out_jobs,
        window,
        origin,
        meta,
        work,
        block,
        span,
    )
    copies = [
        pltpu.make_async_copy(out_jobs.at[job], out.at[pl.ds(job * rows, rows)], sems.at[job])
        for job in range(jobs)
    ]
    for copy in copies:
        copy.start()
    for copy in copies:
        copy.wait()


def shards_whole(meta, queries, keys, values, span):
    block, jobs = queries.shape[0], lax.axis_size("kvh")
    rows = block // jobs
    heads = []
    for which in range(keys.shape[1] // HEAD_WIDTH):
        at = slice(which * HEAD_WIDTH, (which + 1) * HEAD_WIDTH)
        item = jnp.concatenate([keys[:, at], values[:, at]], 1)
        gathered = lax.all_gather(item, "seq", axis=0, tiled=True)
        heads.append(
            pl.pallas_call(
                lambda *refs, which=which: whole_kernel(*refs, which=which, block=block, span=span),
                out_shape=jax.ShapeDtypeStruct((block, GROUP_WIDTH), jnp.bfloat16),
                grid_spec=pltpu.PrefetchScalarGridSpec(
                    num_scalar_prefetch=1,
                    grid=(),
                    in_specs=[pl.BlockSpec(memory_space=pltpu.HBM)] * 2,
                    out_specs=pl.BlockSpec(memory_space=pltpu.HBM),
                    scratch_shapes=[
                        pltpu.VMEM((span * block, 2 * HEAD_WIDTH), jnp.bfloat16),
                        pltpu.VMEM((jobs, rows, GROUP_WIDTH), jnp.bfloat16),
                        pltpu.VMEM((jobs, rows, GROUP_WIDTH), jnp.bfloat16),
                        pltpu.SemaphoreType.DMA((jobs + span,)),
                        *buffers_for(rows, span, block),
                    ],
                ),
                compiler_params=pltpu.CompilerParams(vmem_limit_bytes=VMEM_LIMIT),
            )(meta, queries, gathered)
        )
    return lax.all_to_all(
        jnp.concatenate(heads, 1), "kvh", split_axis=0, concat_axis=1, tiled=True
    )


def shards(queries, keys, values, answer_lengths):
    block = queries.shape[0]
    count, groups = lax.axis_size("seq"), lax.axis_size("kvh")
    span = min(12, count // 2)
    mine, group = lax.axis_index("seq"), lax.axis_index("kvh")
    meta = jnp.concatenate([jnp.stack([mine, group]).astype(jnp.int32), answer_lengths])
    if groups != 2 or span != 8 or count % 4 or keys.shape[1] != 4 * HEAD_WIDTH:
        return shards_whole(meta, queries, keys, values, span)
    core = lax.rem(mine, 2)
    rows = block // groups

    def theirs(value):
        width = value.shape[1] // 2
        return lax.dynamic_slice_in_dim(value, (1 - core) * width, width, 1)

    def permute(value, pairs):
        return lax.ppermute(value, "seq", pairs)

    swap = [(i, i ^ 1) for i in range(count)]
    def chips_ahead(chips):
        return [(i, i + 2 * chips) for i in range(count - 2 * chips)]

    ahead = chips_ahead(2)
    rightward = [(i, i + 2) for i in range(count) if i % 4 < 2]
    leftward = [(i, i - 2) for i in range(count) if i % 4 >= 2]

    their_queries = permute(queries, swap)
    their_kv = permute(jnp.concatenate([theirs(keys), theirs(values)], 1), swap)

    def gather(own):
        near = permute(own, ahead)
        far = permute(near, ahead)
        side_own = permute(own, rightward)
        side_near = permute(near, rightward + leftward)
        side_far = permute(far, leftward)
        return [own, near, far, side_own, side_near, side_far]

    def send(value, flip_core, flip_group):
        pairs = [
            (i * groups + r, (i ^ flip_core) * groups + (r ^ flip_group))
            for i in range(count)
            for r in range(groups)
        ]
        return lax.ppermute(value, ("seq", "kvh"), pairs)

    def run(pieces, earlier, flip_half, which, jobs, placed=()):
        return attend_pair(
            meta,
            queries,
            their_queries,
            pieces,
            placed,
            earlier,
            flip_half,
            which,
            jobs,
            rows,
            span,
        )

    own_first, own_second, upper = own_items(meta, keys, values, their_kv)
    pieces = gather(own_first)
    own, upper = after((own_second, upper), pieces[2:5])
    later = [own] + [permute(own, chips_ahead(n)) for n in (1, 2, 3)] + [permute(upper, chips_ahead(4))]
    far_a, across_a, beside_a, own_a = run(pieces, (), 1, 0, 4)
    got_far_a = send(far_a, 1, 1)
    got_across_a = send(across_a, 0, 1)
    got_beside_a = send(beside_a, 1, 0)
    far_b, across_b = run(later, (beside_a,), 1, 1, 2)
    got_far_b = send(far_b, 1, 1)
    got_across_b = send(across_b, 0, 1)
    placed = (own_a, got_beside_a, got_across_a, got_far_a)
    beside_b, out = run(later, (far_b,), 0, 1, 2, placed)
    got_beside_b = send(beside_b, 1, 0)
    out = place(meta, [got_far_b, got_across_b], (3, 2), 1, out)
    return place(meta, [got_beside_b], (1,), 1, out)


def solution(mesh):
    in_specs = (P("seq", "kvh"), P("seq", "kvh"), P("seq", "kvh"), P())
    out_specs = P(("seq", "kvh"), None)
    return jax.shard_map(shards, mesh=mesh, in_specs=in_specs, out_specs=out_specs, check_vma=False)
```

profile of v0, /device:TPU:21, one launch (start us, length us, event | category | flops | bytes accessed | tf_op | source)
XLA Modules:
  0.0 371.5 jit_solution(14819538774959798279)
XLA Ops:
  0.0 0.7 collective-permute-start
  0.7 1.0 constant_dynamic-slice_fusion
  1.8 1.3 pad_add_fusion.meta.refs_0_
  3.1 3.3 collective-permute-done.1.theirs
  6.3 0.7 copy-done.6
  7.0 2.6 shard_map.46
  9.6 3.2 collective-permute-start.2
  12.8 6.4 %collective-permute-done.2.refs_4_ = bf16[512,256]{1,0:T(8,128)(2,1)S(1)} collective-permute-done((bf16[512,256]{1,0:T(8,128)(2,1)}, bf16[512,256]{1,0:T(8,128)(2,1)S(1)}, u32[]{:S(2)}, u32[]{:S(2)}) %collective-permute-start.2) | collective-permute-done | bytes 262176 | tf_op jit(solution)/shard_map/ppermute | solution.py:538
  19.3 3.2 collective-permute-start.3
  22.5 3.1 collective-permute-start.4
  25.7 2.1 collective-permute-done.3.refs_2_.refs_5_
  27.7 1.3 collective-permute-start.10
  29.0 1.0 collective-permute-done.4.refs_3_.refs_6_
  30.0 5.5 %collective-permute-done.5.refs_4_.refs_7_ = bf16[512,256]{1,0:T(8,128)(2,1)S(1)} collective-permute-done((bf16[512,256]{1,0:T(8,128)(2,1)S(1)}, bf16[512,256]{1,0:T(8,128)(2,1)S(1)}, u32[]{:S(2)}, u32[]{:S(2)}) %collective-permute-start.5) | collective-permute-done | bytes 262176 | tf_op jit(solution)/shard_map/ppermute | solution.py:538
  35.5 0.7 copy-done.3
  36.2 3.5 collective-permute-start.8
  39.7 1.9 collective-permute-start.7
  41.6 1.9 collective-permute-start.6
  43.6 1.3 collective-permute-start.9
  44.9 112.9 %shard_map.48 = (bf16[128,1536]{1,0:T(8,128)(2,1)}, bf16[128,1536]{1,0:T(8,128)(2,1)}, bf16[128,1536]{1,0:T(8,128)(2,1)}, bf16[128,1536]{1,0:T(8,128)(2,1)}) custom-call(s32[6]{0:T(128)} %pad_add_fusion.meta.refs_0_, bf16[256,6144]{1,0:T(8,128)(2,1)} %refs_1_.5, bf16[256,6144]{1,0:T(8,128)(2,1)} %collective-permute-done.refs_2_, ...), custom_call_target="tpu_custom_call" | custom-call | flops 400000000 | bytes 400000 | tf_op jit(solution)/shard_map/pallas_call | solution.py:349
  157.8 0.3 collective-permute-start.12
  158.1 4.1 %collective-permute-start.13 = (bf16[128,1536]{1,0:T(8,128)(2,1)}, bf16[128,1536]{1,0:T(8,128)(2,1)S(1)}, u32[]{:S(2)}, u32[]{:S(2)}) collective-permute-start(bf16[128,1536]{1,0:T(8,128)(2,1)} %get-tuple-element.26), channel_id=1, source_target_pairs={{0,3},{1,2},{2,1},{3,0},{4,7},{5,6},{6,5},{7,4},{8,11},{9,10},{10,... | collective-permute-start | bytes 1179656 | tf_op jit(solution)/shard_map/ppermute | solution.py:565
  162.2 0.7 copy-done.10
  163.0 15.0 %shard_map.49 = (bf16[128,1536]{1,0:T(8,128)(2,1)}, bf16[128,1536]{1,0:T(8,128)(2,1)}) custom-call(s32[6]{0:T(128)} %pad_add_fusion.meta.refs_0_, bf16[256,6144]{1,0:T(8,128)(2,1)} %refs_1_.5, bf16[256,6144]{1,0:T(8,128)(2,1)} %collective-permute-done.refs_2_, bf16[512,256]{1,0:T(8,128)(2,1)} %get-tuple-element.21.refs_3_, ...), custom_call_target="tpu_custom_call" | custom-call | flops 8000000000 | bytes 400000 | tf_op jit(solution)/shard_map/pallas_call | solution.py:349
  178.0 86.3 %collective-permute-start.16 = (bf16[128,1536]{1,0:T(8,128)(2,1)}, bf16[128,1536]{1,0:T(8,128)(2,1)S(1)}, u32[]{:S(2)}, u32[]{:S(2)}) collective-permute-start(bf16[128,1536]{1,0:T(8,128)(2,1)} %get-tuple-element.29), channel_id=1, source_target_pairs={{0,1},{1,0},{2,3},{3,2},{4,5},{5,4},{6,7},{7,6},{8,9},{9,8},{10,11... | collective-permute-start | bytes 1179656 | tf_op jit(solution)/shard_map/ppermute | solution.py:565
  264.4 0.4 collective-permute-start.15
  264.8 0.7 copy-done.7
  265.5 0.2 copy-done.8
  265.8 101.8 %shard_map.50 = (bf16[128,1536]{1,0:T(8,128)(2,1)}, bf16[128,12288]{1,0:T(8,128)(2,1)}) custom-call(s32[6]{0:T(128)} %pad_add_fusion.meta.refs_0_, bf16[256,6144]{1,0:T(8,128)(2,1)} %refs_1_.5, bf16[256,6144]{1,0:T(8,128)(2,1)} %collective-permute-done.refs_2_, bf16[512,256]{1,0:T(8,128)(2,1)} %get-tuple-element.21.refs_3_, ...), custom_call_target="tpu_custom_call" | custom-call | flops 8000000000 | bytes 400000 | tf_op jit(solution)/shard_map/pallas_call | solution.py:349
  367.5 0.4 collective-permute-start.14
  367.9 1.8 shard_map.51.refs_2_
  369.8 1.5 shard_map.52
  (38 shorter events, 0.5 us)
Async XLA Ops:
  0.0 44.9 %collective-permute-start = (bf16[256,6144]{1,0:T(8,128)(2,1)}, bf16[256,6144]{1,0:T(8,128)(2,1)}, u32[]{:S(2)}, u32[]{:S(2)}) collective-permute-start(bf16[256,6144]{1,0:T(8,128)(2,1)} %refs_1_.5), channel_id=1, source_target_pairs={{0,2},{2,0},{4,6},{6,4},{8,10},{10,8},{12,14},{14,12},{16,18},{18,... | collective-permute-start | bytes 9437192 | tf_op jit(solution)/shard_map/ppermute | solution.py:538
  1.7 4.6 %collective-permute-start.1 = (bf16[256,512]{1,0:T(8,128)(2,1)S(1)}, bf16[256,512]{1,0:T(8,128)(2,1)S(1)}, u32[]{:S(2)}, u32[]{:S(2)}) collective-permute-start(bf16[256,512]{1,0:T(8,128)(2,1)S(1)} %pad_maximum_fusion), channel_id=1, source_target_pairs={{0,2},{2,0},{4,6},{6,4},{8,10},{10,8},{12,14},{14,12},{16,18},{18,... | collective-permute-start | bytes 786440 | tf_op jit(solution)/shard_map/ppermute | solution.py:538
  6.3 0.7 copy-start.6
  9.6 9.6 %collective-permute-start.2 = (bf16[512,256]{1,0:T(8,128)(2,1)}, bf16[512,256]{1,0:T(8,128)(2,1)S(1)}, u32[]{:S(2)}, u32[]{:S(2)}) collective-permute-start(bf16[512,256]{1,0:T(8,128)(2,1)} %get-tuple-element.20.refs_3_), channel_id=1, source_target_pairs={{0,8},{2,10},{4,12},{6,14},{8,16},{10,18},{12,20},{14,22},{16,24},... | collective-permute-start | bytes 786440 | tf_op jit(solution)/shard_map/ppermute | solution.py:538
  19.3 25.6 %copy-start.4 = (bf16[512,256]{1,0:T(8,128)(2,1)}, bf16[512,256]{1,0:T(8,128)(2,1)S(1)}, u32[]{:S(2)}) copy-start(bf16[512,256]{1,0:T(8,128)(2,1)S(1)} %collective-permute-done.2.refs_4_) | copy-start | bytes 786436
  19.3 8.5 %collective-permute-start.3 = (bf16[512,256]{1,0:T(8,128)(2,1)S(1)}, bf16[512,256]{1,0:T(8,128)(2,1)S(1)}, u32[]{:S(2)}, u32[]{:S(2)}) collective-permute-start(bf16[512,256]{1,0:T(8,128)(2,1)S(1)} %collective-permute-done.2.refs_4_), channel_id=1, source_target_pairs={{0,8},{2,10},{4,12},{6,14},{8,16},{10,18},{12,20},{14,22},{16,24},... | collective-permute-start | bytes 786440 | tf_op jit(solution)/shard_map/ppermute | solution.py:538
  22.5 7.5 %collective-permute-start.4 = (bf16[512,256]{1,0:T(8,128)(2,1)}, bf16[512,256]{1,0:T(8,128)(2,1)S(1)}, u32[]{:S(2)}, u32[]{:S(2)}) collective-permute-start(bf16[512,256]{1,0:T(8,128)(2,1)} %get-tuple-element.20.refs_3_), channel_id=1, source_target_pairs={{0,4},{2,6},{8,12},{10,14},{16,20},{18,22},{24,28},{26,30},{1,5},{... | collective-permute-start | bytes 786440 | tf_op jit(solution)/shard_map/ppermute | solution.py:538
  25.6 9.9 %collective-permute-start.5 = (bf16[512,256]{1,0:T(8,128)(2,1)S(1)}, bf16[512,256]{1,0:T(8,128)(2,1)S(1)}, u32[]{:S(2)}, u32[]{:S(2)}) collective-permute-start(bf16[512,256]{1,0:T(8,128)(2,1)S(1)} %collective-permute-done.2.refs_4_), channel_id=1, source_target_pairs={{0,4},{2,6},{8,12},{10,14},{16,20},{18,22},{24,28},{26,30},{4,0},{... | collective-permute-start | bytes 786440 | tf_op jit(solution)/shard_map/ppermute | solution.py:538
  27.7 7.8 %copy-start.1 = (bf16[512,256]{1,0:T(8,128)(2,1)}, bf16[512,256]{1,0:T(8,128)(2,1)S(1)}, u32[]{:S(2)}) copy-start(bf16[512,256]{1,0:T(8,128)(2,1)S(1)} %collective-permute-done.3.refs_2_.refs_5_) | copy-start | bytes 786436
  27.7 15.8 %collective-permute-start.10 = (bf16[512,256]{1,0:T(8,128)(2,1)S(1)}, bf16[512,256]{1,0:T(8,128)(2,1)S(1)}, u32[]{:S(2)}, u32[]{:S(2)}) collective-permute-start(bf16[512,256]{1,0:T(8,128)(2,1)S(1)} %collective-permute-done.3.refs_2_.refs_5_), channel_id=1, source_target_pairs={{4,0},{6,2},{12,8},{14,10},{20,16},{22,18},{28,24},{30,26},{5,1},{... | collective-permute-start | bytes 786440 | tf_op jit(solution)/shard_map/ppermute | solution.py:538
  30.0 5.5 %copy-start.2 = (bf16[512,256]{1,0:T(8,128)(2,1)}, bf16[512,256]{1,0:T(8,128)(2,1)S(1)}, u32[]{:S(2)}) copy-start(bf16[512,256]{1,0:T(8,128)(2,1)S(1)} %collective-permute-done.4.refs_3_.refs_6_) | copy-start | bytes 786436
  35.5 0.7 copy-start.3
  36.2 126.0 %collective-permute-start.8 = (bf16[512,256]{1,0:T(8,128)(2,1)}, bf16[512,256]{1,0:T(8,128)(2,1)S(1)}, u32[]{:S(2)}, u32[]{:S(2)}) collective-permute-start(bf16[512,256]{1,0:T(8,128)(2,1)} %get-tuple-element.21.refs_3_), channel_id=1, source_target_pairs={{0,12},{2,14},{4,16},{6,18},{8,20},{10,22},{12,24},{14,26},{16,28}... | collective-permute-start | bytes 786440 | tf_op jit(solution)/shard_map/ppermute | solution.py:538
  39.7 122.5 %collective-permute-start.7 = (bf16[512,256]{1,0:T(8,128)(2,1)}, bf16[512,256]{1,0:T(8,128)(2,1)S(1)}, u32[]{:S(2)}, u32[]{:S(2)}) collective-permute-start(bf16[512,256]{1,0:T(8,128)(2,1)} %get-tuple-element.21.refs_3_), channel_id=1, source_target_pairs={{0,8},{2,10},{4,12},{6,14},{8,16},{10,18},{12,20},{14,22},{16,24},... | collective-permute-start | bytes 786440 | tf_op jit(solution)/shard_map/ppermute | solution.py:538
  41.6 120.6 %collective-permute-start.6 = (bf16[512,256]{1,0:T(8,128)(2,1)}, bf16[512,256]{1,0:T(8,128)(2,1)}, u32[]{:S(2)}, u32[]{:S(2)}) collective-permute-start(bf16[512,256]{1,0:T(8,128)(2,1)} %get-tuple-element.21.refs_3_), channel_id=1, source_target_pairs={{0,4},{2,6},{4,8},{6,10},{8,12},{10,14},{12,16},{14,18},{16,20},{1... | collective-permute-start | bytes 786440 | tf_op jit(solution)/shard_map/ppermute | solution.py:538
  43.6 1.3 copy-start.5
  43.6 114.5 %collective-permute-start.9 = (bf16[256,256]{1,0:T(8,128)(2,1)}, bf16[256,256]{1,0:T(8,128)(2,1)S(1)}, u32[]{:S(2)}, u32[]{:S(2)}) collective-permute-start(bf16[256,256]{1,0:T(8,128)(2,1)} %get-tuple-element.22), channel_id=1, source_target_pairs={{0,16},{2,18},{4,20},{6,22},{8,24},{10,26},{12,28},{14,30},{1,17},... | collective-permute-start | bytes 393224 | tf_op jit(solution)/shard_map/ppermute | solution.py:538
  157.8 106.9 %collective-permute-start.12 = (bf16[128,1536]{1,0:T(8,128)(2,1)}, bf16[128,1536]{1,0:T(8,128)(2,1)S(1)}, u32[]{:S(2)}, u32[]{:S(2)}) collective-permute-start(bf16[128,1536]{1,0:T(8,128)(2,1)} %get-tuple-element.25), channel_id=1, source_target_pairs={{0,1},{1,0},{2,3},{3,2},{4,5},{5,4},{6,7},{7,6},{8,9},{9,8},{10,11... | collective-permute-start | bytes 1179656 | tf_op jit(solution)/shard_map/ppermute | solution.py:565
  158.1 4.1 %copy-start.12 = (bf16[256,256]{1,0:T(8,128)(2,1)}, bf16[256,256]{1,0:T(8,128)(2,1)S(1)}, u32[]{:S(2)}) copy-start(bf16[256,256]{1,0:T(8,128)(2,1)S(1)} %collective-permute-done.9.refs_7_) | copy-start | bytes 393220
  158.1 106.6 %collective-permute-start.13 = (bf16[128,1536]{1,0:T(8,128)(2,1)}, bf16[128,1536]{1,0:T(8,128)(2,1)S(1)}, u32[]{:S(2)}, u32[]{:S(2)}) collective-permute-start(bf16[128,1536]{1,0:T(8,128)(2,1)} %get-tuple-element.26), channel_id=1, source_target_pairs={{0,3},{1,2},{2,1},{3,0},{4,7},{5,6},{6,5},{7,4},{8,11},{9,10},{10,... | collective-permute-start | bytes 1179656 | tf_op jit(solution)/shard_map/ppermute | solution.py:565
  162.2 0.7 copy-start.10
  162.2 102.5 %collective-permute-start.11 = (bf16[128,1536]{1,0:T(8,128)(2,1)}, bf16[128,1536]{1,0:T(8,128)(2,1)S(1)}, u32[]{:S(2)}, u32[]{:S(2)}) collective-permute-start(bf16[128,1536]{1,0:T(8,128)(2,1)} %get-tuple-element.24.refs_8_), channel_id=1, source_target_pairs={{0,2},{1,3},{2,0},{3,1},{4,6},{5,7},{6,4},{7,5},{8,10},{9,11},{10,... | collective-permute-start | bytes 1179656 | tf_op jit(solution)/shard_map/ppermute | solution.py:565
  162.2 0.8 copy-start.11
  178.0 189.9 %collective-permute-start.16 = (bf16[128,1536]{1,0:T(8,128)(2,1)}, bf16[128,1536]{1,0:T(8,128)(2,1)S(1)}, u32[]{:S(2)}, u32[]{:S(2)}) collective-permute-start(bf16[128,1536]{1,0:T(8,128)(2,1)} %get-tuple-element.29), channel_id=1, source_target_pairs={{0,1},{1,0},{2,3},{3,2},{4,5},{5,4},{6,7},{7,6},{8,9},{9,8},{10,11... | collective-permute-start | bytes 1179656 | tf_op jit(solution)/shard_map/ppermute | solution.py:565
  264.4 103.6 %collective-permute-start.15 = (bf16[128,1536]{1,0:T(8,128)(2,1)}, bf16[128,1536]{1,0:T(8,128)(2,1)S(1)}, u32[]{:S(2)}, u32[]{:S(2)}) collective-permute-start(bf16[128,1536]{1,0:T(8,128)(2,1)} %get-tuple-element.27.refs_12_), channel_id=1, source_target_pairs={{0,3},{1,2},{2,1},{3,0},{4,7},{5,6},{6,5},{7,4},{8,11},{9,10},{10,... | collective-permute-start | bytes 1179656 | tf_op jit(solution)/shard_map/ppermute | solution.py:565
  264.7 0.8 copy-start.7
  264.7 0.9 copy-start.8
  264.7 1.0 copy-start.9
  265.8 102.2 %copy-start = (s32[6]{0:T(128)S(1)}, s32[6]{0:T(128)}, u32[]{:S(2)}) copy-start(s32[6]{0:T(128)} %pad_add_fusion.meta.refs_0_) | copy-start | bytes 76
  367.5 2.2 collective-permute-start.14
where the time goes:
time: 371 us
  Pallas kernels  236 us (64%)
  starting transfers between devices  112 us (30%)
  waiting for transfers between devices  18.2 us (5%)
  local copies, waits for them, and re-layouts  4.19 us (1%)
    pallas_call x3, Pallas kernels, attend_pair(): pl.pallas_call(lambda *refs: pair_kernel(*refs, flip_half=flip_half, whic...  230 us
    ppermute x6, starting transfers between devices, send(): return lax.ppermute(value, ('seq', 'kvh'), pairs)  91.5 us
    ppermute x11, starting transfers between devices, permute(): return lax.ppermute(value, 'seq', pairs)  20.2 us
    ppermute x11, waiting for transfers between devices, permute(): return lax.ppermute(value, 'seq', pairs)  18.2 us
  transfers between devices with their start and end apart: 17, of which 5 were waited for; matrix products, arithmetic and copies ran while one was open for 1% of the time, Pallas kernels for 63%

commit v1 on v0

--- a/solution.py
+++ b/solution.py
@@ -32,7 +32,7 @@
 def attend_rows(count, offset, q_ref, out_ref, work, block):
     rows = q_ref.shape[0]
     stacked = STACK * rows
-    window, nearest, probs, stack, staged, facing = work[:6]
+    window, nearest, shift, probs, stack, staged, facing = work[:7]
     width = count * block
     first = window.shape[0] - width
     tokens = lax.rem(lax.broadcasted_iota(jnp.int32, (stacked, block), 0), rows) + offset
@@ -40,29 +40,26 @@
 
     def load(number):
         for h in range(STACK):
-            stack[h * rows : (h + 1) * rows, :HEAD_WIDTH] = q_ref[:, lanes(number * STACK + h)]
+            stack[h * rows : (h + 1) * rows, :] = q_ref[:, lanes(number * STACK + h)]
 
     def score(slot):
-        keys = window[first + slot * block : first + (slot + 1) * block, : 2 * HEAD_WIDTH]
+        keys = window[first + slot * block : first + (slot + 1) * block, :HEAD_WIDTH]
         return lax.dot_general(
             stack[...], keys, (((1,), (1,)), ((), ())), preferred_element_type=jnp.float32
         )
 
     def begin():
-        ones = window[first : first + HEAD_WIDTH, HEAD_WIDTH : 2 * HEAD_WIDTH]
-        column = lax.broadcasted_iota(jnp.int32, (rows, HEAD_WIDTH), 1)
+        nearest[...] = jnp.where(mask, score(count - 1), -1e30)
         for h in range(STACK):
             at = slice(h * rows, (h + 1) * rows)
-            same = jnp.dot(
-                stack[at, :HEAD_WIDTH] * facing[...], ones, preferred_element_type=jnp.float32
-            )
-            stack[at, HEAD_WIDTH:] = jnp.where(column == 0, -same, 0.0).astype(stack.dtype)
-        nearest[...] = jnp.where(mask, score(count - 1), -1e30)
+            ones = window[first : first + HEAD_WIDTH, 2 * HEAD_WIDTH :]
+            same = jnp.dot(stack[at, :] * facing[...], ones, preferred_element_type=jnp.float32)
+            shift[at, :] = same * SCALE_LOG2
 
     def soften(found, slot):
         for piece in range(block // HEAD_WIDTH):
             at = slice(piece * HEAD_WIDTH, (piece + 1) * HEAD_WIDTH)
-            weights = jnp.exp2(found[:, at] * SCALE_LOG2)
+            weights = jnp.exp2(found[:, at] * SCALE_LOG2 - shift[...])
             start = slot * block + piece * HEAD_WIDTH
             probs[:, start : start + HEAD_WIDTH] = weights.astype(jnp.bfloat16)
 
@@ -79,10 +76,10 @@
         found = jnp.dot(
             probs[:, :width], window[first:, HEAD_WIDTH:], preferred_element_type=jnp.float32
         )
-        total = found[:, :HEAD_WIDTH]
+        total = found[:, HEAD_WIDTH:]
         guess = pl.reciprocal(total, approx=True)
         guess = guess * (2.0 - total * guess)
-        staged[...] = (found[:, HEAD_WIDTH:] * guess).astype(staged.dtype)
+        staged[...] = (found[:, :HEAD_WIDTH] * guess).astype(staged.dtype)
         return total
 
     def release(number):
@@ -107,7 +104,7 @@
 
 def attend_rows_wide(visible, offset, q_ref, out_ref, work, block):
     rows = q_ref.shape[0]
-    window, (peak, total, blended) = work[0], work[6:9]
+    window, (peak, total, blended) = work[0], work[7:10]
     last = window.shape[0] - block
     tokens = lax.broadcasted_iota(jnp.int32, (rows, block), 0) + offset
     columns = lax.broadcasted_iota(jnp.int32, (rows, block), 1)
@@ -136,7 +133,7 @@
             total[...] = total[...] * shrink + jnp.sum(weights, axis=-1, keepdims=True)
             blended[...] = blended[...] * shrink + jnp.dot(
                 weights.astype(jnp.bfloat16),
-                window[at, 2 * HEAD_WIDTH :],
+                window[at, HEAD_WIDTH : 2 * HEAD_WIDTH],
                 preferred_element_type=jnp.float32,
             )
 
@@ -148,8 +145,9 @@
     return [
         pltpu.VMEM((span * block, 3 * HEAD_WIDTH), jnp.bfloat16),
         pltpu.VMEM((stacked, block), jnp.float32),
+        pltpu.VMEM((stacked, HEAD_WIDTH), jnp.float32),
         pltpu.VMEM((stacked, span * block), jnp.bfloat16),
-        pltpu.VMEM((stacked, 2 * HEAD_WIDTH), jnp.bfloat16),
+        pltpu.VMEM((stacked, HEAD_WIDTH), jnp.bfloat16),
         pltpu.VMEM((stacked, HEAD_WIDTH), jnp.bfloat16),
         pltpu.VMEM((rows, HEAD_WIDTH), jnp.bfloat16),
         pltpu.VMEM((rows, HEAD_WIDTH), jnp.float32),
@@ -159,22 +157,23 @@
     ]
 
 
-WORK = 10
-
-
-def attend_jobs(jobs, position_of, q_jobs, out_jobs, arrived, origin, meta, work, block, span, done=None):
-    work[0][:, HEAD_WIDTH : 2 * HEAD_WIDTH] = jnp.ones((span * block, HEAD_WIDTH), jnp.bfloat16)
+WORK = 11
+
+
+def attend_jobs(jobs, position_of, q_jobs, out_jobs, arrived, origin, meta, work, block, span, ready=None, done=None):
+    work[0][:, 2 * HEAD_WIDTH :] = jnp.ones((span * block, HEAD_WIDTH), jnp.bfloat16)
 
     @pl.loop(0, jobs)
     def _(job):
+        if ready is not None:
+            ready(job)
         index, offset = position_of(job)
         start = lax.div(first_visible(meta, index * block), block)
         visible = index - start + 1
         last = (index - origin + 1 - span) * block
-        window, facing, most = work[0], work[5], work[9]
+        window, facing, most = work[0], work[6], work[10]
         moved = pl.ds(pl.multiple_of(last, block), span * block)
-        window[:, :HEAD_WIDTH] = arrived[moved, :HEAD_WIDTH]
-        window[:, 2 * HEAD_WIDTH :] = arrived[moved, HEAD_WIDTH:]
+        window[:, : 2 * HEAD_WIDTH] = arrived[moved, :]
         here = pl.ds(pl.multiple_of(last + (span - 1) * block + offset, facing.shape[0]), facing.shape[0])
         facing[...] = arrived[here, :HEAD_WIDTH]
         for count in range(1, span + 1):
@@ -282,10 +281,11 @@
             (fill(side_far, 0, 1, 2 * block, 3), fill(side_near, 0, 1, 2 * block, 3)),
             (fill(side_near, 0, 5, 2 * block, 4), fill(side_own, 0, 5, 2 * block, 4)),
         ]
+    queries_in = []
     for job in range(jobs):
         source = queries if job % 2 else theirs
         at = pl.ds(pl.multiple_of((2 * core + which) * GROUP_WIDTH, GROUP_WIDTH), GROUP_WIDTH)
-        fixed.append(
+        queries_in.append(
             pltpu.make_async_copy(
                 source.at[pl.ds(pl.multiple_of(half_of(job) * rows, rows), rows), at],
                 q_jobs.at[job],
@@ -297,6 +297,8 @@
     for on_left, on_right in by_side:
         pl.when(right == 0)(on_left.start)
         pl.when(right == 1)(on_right.start)
+    for copy in queries_in:
+        copy.start()
     for copy in fixed:
         copy.wait()
     for on_left, _ in by_side:
@@ -321,12 +323,16 @@
         for job, out in enumerate(targets)
     ]
 
+    def ready(job):
+        for number, copy in enumerate(queries_in):
+            pl.when(job == number)(copy.wait)
+
     def done(job):
         for number, copy in enumerate(copies):
             pl.when(job == number)(copy.start)
 
     attend_jobs(
-        jobs, position_of, q_jobs, out_jobs, window, origin, meta, work, block, span, done
+        jobs, position_of, q_jobs, out_jobs, window, origin, meta, work, block, span, ready, done
     )
     for load, store in zip(loads, stores):
         load.wait()
@@ -581,7 +587,7 @@
 
     own_first, own_second, upper = own_items(meta, keys, values, their_kv)
     pieces = gather(own_first)
-    own, upper = after((own_second, upper), pieces[2:5])
+    own, upper = after((own_second, upper), pieces[2:4])
     later = [own] + [permute(own, chips_ahead(n)) for n in (1, 2, 3)] + [permute(upper, chips_ahead(4))]
     far_a, across_a, beside_a, own_a = run(pieces, (), 1, 0, 4)
     got_far_a = send(far_a, 1, 1)

time: 371 us -> 366 us (0.987)
  the two profiles are of different devices: /device:TPU:21 before, /device:TPU:29 now
where the time goes in v1:
time: 366 us
  Pallas kernels  233 us (64%)
  starting transfers between devices  110 us (30%)
  waiting for transfers between devices  17.1 us (5%)
  local copies, waits for them, and re-layouts  4.18 us (1%)
    pallas_call x3, Pallas kernels, attend_pair(): pl.pallas_call(lambda *refs: pair_kernel(*refs, flip_half=flip_half, whic...  228 us
    ppermute x6, starting transfers between devices, send(): return lax.ppermute(value, ('seq', 'kvh'), pairs)  94 us
    ppermute x11, waiting for transfers between devices, permute(): return lax.ppermute(value, 'seq', pairs)  17.1 us
    ppermute x11, starting transfers between devices, permute(): return lax.ppermute(value, 'seq', pairs)  15.8 us
  transfers between devices with their start and end apart: 17, of which 4 were waited for; matrix products, arithmetic and copies ran while one was open for 1% of the time, Pallas kernels for 63%

profile of v1, /device:TPU:29, one launch (start us, length us, event | category | flops | bytes accessed | tf_op | source)
XLA Modules:
  0.0 366.3 jit_solution(3388639213137882908)
XLA Ops:
  0.0 0.7 collective-permute-start
  0.7 1.0 constant_dynamic-slice_fusion
  1.8 1.3 pad_add_fusion.meta.refs_0_
  3.1 3.3 collective-permute-done.1.theirs
  6.3 0.7 copy-done.6
  7.0 2.6 shard_map.46
  9.6 1.3 collective-permute-start.2
  10.9 8.3 %collective-permute-done.2.refs_4_ = bf16[512,256]{1,0:T(8,128)(2,1)S(1)} collective-permute-done((bf16[512,256]{1,0:T(8,128)(2,1)}, bf16[512,256]{1,0:T(8,128)(2,1)S(1)}, u32[]{:S(2)}, u32[]{:S(2)}) %collective-permute-start.2) | collective-permute-done | bytes 262176 | tf_op jit(solution)/shard_map/ppermute | solution.py:544
  19.3 1.3 collective-permute-start.3
  20.5 3.1 collective-permute-start.4
  23.8 4.0 %collective-permute-done.3.refs_2_.refs_5_ = bf16[512,256]{1,0:T(8,128)(2,1)S(1)} collective-permute-done((bf16[512,256]{1,0:T(8,128)(2,1)S(1)}, bf16[512,256]{1,0:T(8,128)(2,1)S(1)}, u32[]{:S(2)}, u32[]{:S(2)}) %collective-permute-start.3) | collective-permute-done | bytes 262176 | tf_op jit(solution)/shard_map/ppermute | solution.py:544
  27.7 1.3 collective-permute-start.10
  29.1 0.7 copy-done.2
  29.8 1.3 collective-permute-start.7
  31.0 1.3 collective-permute-start.6
  32.3 1.5 collective-permute-done.9.refs_7_
  33.9 4.1 %collective-permute-start.5 = (bf16[512,256]{1,0:T(8,128)(2,1)}, bf16[512,256]{1,0:T(8,128)(2,1)}, u32[]{:S(2)}, u32[]{:S(2)}) collective-permute-start(bf16[512,256]{1,0:T(8,128)(2,1)} %get-tuple-element.21.refs_3_), channel_id=1, source_target_pairs={{0,4},{2,6},{4,8},{6,10},{8,12},{10,14},{12,16},{14,18},{16,20},{1... | collective-permute-start | bytes 786440 | tf_op jit(solution)/shard_map/ppermute | solution.py:544
  38.0 1.3 collective-permute-start.8
  39.3 111.9 %shard_map.48 = (bf16[128,1536]{1,0:T(8,128)(2,1)}, bf16[128,1536]{1,0:T(8,128)(2,1)}, bf16[128,1536]{1,0:T(8,128)(2,1)}, bf16[128,1536]{1,0:T(8,128)(2,1)}) custom-call(s32[6]{0:T(128)} %pad_add_fusion.meta.refs_0_, bf16[256,6144]{1,0:T(8,128)(2,1)} %refs_1_.5, bf16[256,6144]{1,0:T(8,128)(2,1)} %collective-permute-done.refs_2_, ...), custom_call_target="tpu_custom_call" | custom-call | flops 400000000 | bytes 400000 | tf_op jit(solution)/shard_map/pallas_call | solution.py:355
  151.2 0.3 collective-permute-start.12
  151.5 6.6 %collective-permute-start.13 = (bf16[128,1536]{1,0:T(8,128)(2,1)}, bf16[128,1536]{1,0:T(8,128)(2,1)S(1)}, u32[]{:S(2)}, u32[]{:S(2)}) collective-permute-start(bf16[128,1536]{1,0:T(8,128)(2,1)} %get-tuple-element.26), channel_id=1, source_target_pairs={{0,3},{1,2},{2,1},{3,0},{4,7},{5,6},{6,5},{7,4},{8,11},{9,10},{10,... | collective-permute-start | bytes 1179656 | tf_op jit(solution)/shard_map/ppermute | solution.py:571
  158.2 0.7 copy-done.10
  158.9 0.1 copy-done.11
  159.0 14.5 %shard_map.49 = (bf16[128,1536]{1,0:T(8,128)(2,1)}, bf16[128,1536]{1,0:T(8,128)(2,1)}) custom-call(s32[6]{0:T(128)} %pad_add_fusion.meta.refs_0_, bf16[256,6144]{1,0:T(8,128)(2,1)} %refs_1_.5, bf16[256,6144]{1,0:T(8,128)(2,1)} %collective-permute-done.refs_2_, bf16[512,256]{1,0:T(8,128)(2,1)} %get-tuple-element.21.refs_3_, ...), custom_call_target="tpu_custom_call" | custom-call | flops 8000000000 | bytes 400000 | tf_op jit(solution)/shard_map/pallas_call | solution.py:355
  173.5 86.3 %collective-permute-start.16 = (bf16[128,1536]{1,0:T(8,128)(2,1)}, bf16[128,1536]{1,0:T(8,128)(2,1)S(1)}, u32[]{:S(2)}, u32[]{:S(2)}) collective-permute-start(bf16[128,1536]{1,0:T(8,128)(2,1)} %get-tuple-element.29), channel_id=1, source_target_pairs={{0,1},{1,0},{2,3},{3,2},{4,5},{5,4},{6,7},{7,6},{8,9},{9,8},{10,11... | collective-permute-start | bytes 1179656 | tf_op jit(solution)/shard_map/ppermute | solution.py:571
  259.7 0.4 collective-permute-start.15
  260.2 0.7 copy-done.7
  260.9 0.2 copy-done.8
  261.2 101.2 %shard_map.50 = (bf16[128,1536]{1,0:T(8,128)(2,1)}, bf16[128,12288]{1,0:T(8,128)(2,1)}) custom-call(s32[6]{0:T(128)} %pad_add_fusion.meta.refs_0_, bf16[256,6144]{1,0:T(8,128)(2,1)} %refs_1_.5, bf16[256,6144]{1,0:T(8,128)(2,1)} %collective-permute-done.refs_2_, bf16[512,256]{1,0:T(8,128)(2,1)} %get-tuple-element.21.refs_3_, ...), custom_call_target="tpu_custom_call" | custom-call | flops 8000000000 | bytes 400000 | tf_op jit(solution)/shard_map/pallas_call | solution.py:355
  362.4 0.4 collective-permute-start.14
  362.8 1.8 shard_map.51.refs_2_
  364.6 1.5 shard_map.52
  (38 shorter events, 0.3 us)
Async XLA Ops:
  0.0 39.3 %collective-permute-start = (bf16[256,6144]{1,0:T(8,128)(2,1)}, bf16[256,6144]{1,0:T(8,128)(2,1)}, u32[]{:S(2)}, u32[]{:S(2)}) collective-permute-start(bf16[256,6144]{1,0:T(8,128)(2,1)} %refs_1_.5), channel_id=1, source_target_pairs={{0,2},{2,0},{4,6},{6,4},{8,10},{10,8},{12,14},{14,12},{16,18},{18,... | collective-permute-start | bytes 9437192 | tf_op jit(solution)/shard_map/ppermute | solution.py:544
  1.7 4.6 %collective-permute-start.1 = (bf16[256,512]{1,0:T(8,128)(2,1)S(1)}, bf16[256,512]{1,0:T(8,128)(2,1)S(1)}, u32[]{:S(2)}, u32[]{:S(2)}) collective-permute-start(bf16[256,512]{1,0:T(8,128)(2,1)S(1)} %pad_maximum_fusion), channel_id=1, source_target_pairs={{0,2},{2,0},{4,6},{6,4},{8,10},{10,8},{12,14},{14,12},{16,18},{18,... | collective-permute-start | bytes 786440 | tf_op jit(solution)/shard_map/ppermute | solution.py:544
  6.3 0.7 copy-start.6
  9.6 9.6 %collective-permute-start.2 = (bf16[512,256]{1,0:T(8,128)(2,1)}, bf16[512,256]{1,0:T(8,128)(2,1)S(1)}, u32[]{:S(2)}, u32[]{:S(2)}) collective-permute-start(bf16[512,256]{1,0:T(8,128)(2,1)} %get-tuple-element.20.refs_3_), channel_id=1, source_target_pairs={{0,8},{2,10},{4,12},{6,14},{8,16},{10,18},{12,20},{14,22},{16,24},... | collective-permute-start | bytes 786440 | tf_op jit(solution)/shard_map/ppermute | solution.py:544
  19.3 20.1 %copy-start.3 = (bf16[512,256]{1,0:T(8,128)(2,1)}, bf16[512,256]{1,0:T(8,128)(2,1)S(1)}, u32[]{:S(2)}) copy-start(bf16[512,256]{1,0:T(8,128)(2,1)S(1)} %collective-permute-done.2.refs_4_) | copy-start | bytes 786436
  19.3 8.5 %collective-permute-start.3 = (bf16[512,256]{1,0:T(8,128)(2,1)S(1)}, bf16[512,256]{1,0:T(8,128)(2,1)S(1)}, u32[]{:S(2)}, u32[]{:S(2)}) collective-permute-start(bf16[512,256]{1,0:T(8,128)(2,1)S(1)} %collective-permute-done.2.refs_4_), channel_id=1, source_target_pairs={{0,8},{2,10},{4,12},{6,14},{8,16},{10,18},{12,20},{14,22},{16,24},... | collective-permute-start | bytes 786440 | tf_op jit(solution)/shard_map/ppermute | solution.py:544
  20.5 8.5 %collective-permute-start.4 = (bf16[512,256]{1,0:T(8,128)(2,1)}, bf16[512,256]{1,0:T(8,128)(2,1)S(1)}, u32[]{:S(2)}, u32[]{:S(2)}) collective-permute-start(bf16[512,256]{1,0:T(8,128)(2,1)} %get-tuple-element.20.refs_3_), channel_id=1, source_target_pairs={{0,4},{2,6},{8,12},{10,14},{16,20},{18,22},{24,28},{26,30},{1,5},{... | collective-permute-start | bytes 786440 | tf_op jit(solution)/shard_map/ppermute | solution.py:544
  23.7 10.2 %collective-permute-start.9 = (bf16[512,256]{1,0:T(8,128)(2,1)S(1)}, bf16[512,256]{1,0:T(8,128)(2,1)S(1)}, u32[]{:S(2)}, u32[]{:S(2)}) collective-permute-start(bf16[512,256]{1,0:T(8,128)(2,1)S(1)} %collective-permute-done.2.refs_4_), channel_id=1, source_target_pairs={{0,4},{2,6},{8,12},{10,14},{16,20},{18,22},{24,28},{26,30},{4,0},{... | collective-permute-start | bytes 786440 | tf_op jit(solution)/shard_map/ppermute | solution.py:544
  27.7 1.3 copy-start.1
  27.7 10.2 %collective-permute-start.10 = (bf16[512,256]{1,0:T(8,128)(2,1)S(1)}, bf16[512,256]{1,0:T(8,128)(2,1)S(1)}, u32[]{:S(2)}, u32[]{:S(2)}) collective-permute-start(bf16[512,256]{1,0:T(8,128)(2,1)S(1)} %collective-permute-done.3.refs_2_.refs_5_), channel_id=1, source_target_pairs={{4,0},{6,2},{12,8},{14,10},{20,16},{22,18},{28,24},{30,26},{5,1},{... | collective-permute-start | bytes 786440 | tf_op jit(solution)/shard_map/ppermute | solution.py:544
  29.0 0.7 copy-start.2
  29.8 128.4 %collective-permute-start.7 = (bf16[512,256]{1,0:T(8,128)(2,1)}, bf16[512,256]{1,0:T(8,128)(2,1)S(1)}, u32[]{:S(2)}, u32[]{:S(2)}) collective-permute-start(bf16[512,256]{1,0:T(8,128)(2,1)} %get-tuple-element.21.refs_3_), channel_id=1, source_target_pairs={{0,12},{2,14},{4,16},{6,18},{8,20},{10,22},{12,24},{14,26},{16,28}... | collective-permute-start | bytes 786440 | tf_op jit(solution)/shard_map/ppermute | solution.py:544
  31.0 127.1 %collective-permute-start.6 = (bf16[512,256]{1,0:T(8,128)(2,1)}, bf16[512,256]{1,0:T(8,128)(2,1)S(1)}, u32[]{:S(2)}, u32[]{:S(2)}) collective-permute-start(bf16[512,256]{1,0:T(8,128)(2,1)} %get-tuple-element.21.refs_3_), channel_id=1, source_target_pairs={{0,8},{2,10},{4,12},{6,14},{8,16},{10,18},{12,20},{14,22},{16,24},... | collective-permute-start | bytes 786440 | tf_op jit(solution)/shard_map/ppermute | solution.py:544
  33.9 5.5 %copy-start.4 = (bf16[512,256]{1,0:T(8,128)(2,1)}, bf16[512,256]{1,0:T(8,128)(2,1)S(1)}, u32[]{:S(2)}) copy-start(bf16[512,256]{1,0:T(8,128)(2,1)S(1)} %collective-permute-done.9.refs_7_) | copy-start | bytes 786436
  33.9 124.3 %collective-permute-start.5 = (bf16[512,256]{1,0:T(8,128)(2,1)}, bf16[512,256]{1,0:T(8,128)(2,1)}, u32[]{:S(2)}, u32[]{:S(2)}) collective-permute-start(bf16[512,256]{1,0:T(8,128)(2,1)} %get-tuple-element.21.refs_3_), channel_id=1, source_target_pairs={{0,4},{2,6},{4,8},{6,10},{8,12},{10,14},{12,16},{14,18},{16,20},{1... | collective-permute-start | bytes 786440 | tf_op jit(solution)/shard_map/ppermute | solution.py:544
  38.0 1.3 copy-start.5
  38.0 113.5 %collective-permute-start.8 = (bf16[256,256]{1,0:T(8,128)(2,1)}, bf16[256,256]{1,0:T(8,128)(2,1)S(1)}, u32[]{:S(2)}, u32[]{:S(2)}) collective-permute-start(bf16[256,256]{1,0:T(8,128)(2,1)} %get-tuple-element.22), channel_id=1, source_target_pairs={{0,16},{2,18},{4,20},{6,22},{8,24},{10,26},{12,28},{14,30},{1,17},... | collective-permute-start | bytes 393224 | tf_op jit(solution)/shard_map/ppermute | solution.py:544
  151.2 108.9 %collective-permute-start.12 = (bf16[128,1536]{1,0:T(8,128)(2,1)}, bf16[128,1536]{1,0:T(8,128)(2,1)S(1)}, u32[]{:S(2)}, u32[]{:S(2)}) collective-permute-start(bf16[128,1536]{1,0:T(8,128)(2,1)} %get-tuple-element.25), channel_id=1, source_target_pairs={{0,1},{1,0},{2,3},{3,2},{4,5},{5,4},{6,7},{7,6},{8,9},{9,8},{10,11... | collective-permute-start | bytes 1179656 | tf_op jit(solution)/shard_map/ppermute | solution.py:571
  151.5 6.7 %copy-start.12 = (bf16[256,256]{1,0:T(8,128)(2,1)}, bf16[256,256]{1,0:T(8,128)(2,1)S(1)}, u32[]{:S(2)}) copy-start(bf16[256,256]{1,0:T(8,128)(2,1)S(1)} %collective-permute-done.8.refs_7_) | copy-start | bytes 393220
  151.5 108.6 %collective-permute-start.13 = (bf16[128,1536]{1,0:T(8,128)(2,1)}, bf16[128,1536]{1,0:T(8,128)(2,1)S(1)}, u32[]{:S(2)}, u32[]{:S(2)}) collective-permute-start(bf16[128,1536]{1,0:T(8,128)(2,1)} %get-tuple-element.26), channel_id=1, source_target_pairs={{0,3},{1,2},{2,1},{3,0},{4,7},{5,6},{6,5},{7,4},{8,11},{9,10},{10,... | collective-permute-start | bytes 1179656 | tf_op jit(solution)/shard_map/ppermute | solution.py:571
  158.2 0.7 copy-start.10
  158.2 102.0 %collective-permute-start.11 = (bf16[128,1536]{1,0:T(8,128)(2,1)}, bf16[128,1536]{1,0:T(8,128)(2,1)S(1)}, u32[]{:S(2)}, u32[]{:S(2)}) collective-permute-start(bf16[128,1536]{1,0:T(8,128)(2,1)} %get-tuple-element.24.refs_8_), channel_id=1, source_target_pairs={{0,2},{1,3},{2,0},{3,1},{4,6},{5,7},{6,4},{7,5},{8,10},{9,11},{10,... | collective-permute-start | bytes 1179656 | tf_op jit(solution)/shard_map/ppermute | solution.py:571
  158.2 0.8 copy-start.11
  173.5 189.3 %collective-permute-start.16 = (bf16[128,1536]{1,0:T(8,128)(2,1)}, bf16[128,1536]{1,0:T(8,128)(2,1)S(1)}, u32[]{:S(2)}, u32[]{:S(2)}) collective-permute-start(bf16[128,1536]{1,0:T(8,128)(2,1)} %get-tuple-element.29), channel_id=1, source_target_pairs={{0,1},{1,0},{2,3},{3,2},{4,5},{5,4},{6,7},{7,6},{8,9},{9,8},{10,11... | collective-permute-start | bytes 1179656 | tf_op jit(solution)/shard_map/ppermute | solution.py:571
  259.7 103.0 %collective-permute-start.15 = (bf16[128,1536]{1,0:T(8,128)(2,1)}, bf16[128,1536]{1,0:T(8,128)(2,1)S(1)}, u32[]{:S(2)}, u32[]{:S(2)}) collective-permute-start(bf16[128,1536]{1,0:T(8,128)(2,1)} %get-tuple-element.27.refs_12_), channel_id=1, source_target_pairs={{0,3},{1,2},{2,1},{3,0},{4,7},{5,6},{6,5},{7,4},{8,11},{9,10},{10,... | collective-permute-start | bytes 1179656 | tf_op jit(solution)/shard_map/ppermute | solution.py:571
  260.1 0.8 copy-start.7
  260.1 0.9 copy-start.8
  260.1 1.0 copy-start.9
  261.2 101.6 %copy-start = (s32[6]{0:T(128)S(1)}, s32[6]{0:T(128)}, u32[]{:S(2)}) copy-start(s32[6]{0:T(128)} %pad_add_fusion.meta.refs_0_) | copy-start | bytes 76
  362.4 2.3 collective-permute-start.14

commit v2 on v1

--- a/solution.py
+++ b/solution.py
@@ -12,7 +12,7 @@
 GROUP_WIDTH = QUERY_PER_KEY * HEAD_WIDTH
 SCALE_LOG2 = math.log2(math.e) / math.sqrt(HEAD_WIDTH)
 VMEM_LIMIT = 62 * 1024 * 1024
-STACK = 4
+STACK = 6
 STACKS = QUERY_PER_KEY // STACK
 
 

time: 366 us -> 355 us (0.970)
  the two profiles are of different devices: /device:TPU:29 before, /device:TPU:31 now
where the time goes in v2:
time: 355 us; the launch traced here: 362 us
  Pallas kernels  231 us (65%)
  starting transfers between devices  108 us (30%)
  waiting for transfers between devices  17 us (5%)
  local copies, waits for them, and re-layouts  4.18 us (1%)
    pallas_call x3, Pallas kernels, attend_pair(): pl.pallas_call(lambda *refs: pair_kernel(*refs, flip_half=flip_half, whic...  225 us
    ppermute x6, starting transfers between devices, send(): return lax.ppermute(value, ('seq', 'kvh'), pairs)  93.7 us
    ppermute x11, waiting for transfers between devices, permute(): return lax.ppermute(value, 'seq', pairs)  17 us
    ppermute x11, starting transfers between devices, permute(): return lax.ppermute(value, 'seq', pairs)  14.1 us
  transfers between devices with their start and end apart: 17, of which 4 were waited for; matrix products, arithmetic and copies ran while one was open for 1% of the time, Pallas kernels for 63%

profile of v2, /device:TPU:31, one launch (start us, length us, event | category | flops | bytes accessed | tf_op | source)
XLA Modules:
  0.0 361.7 jit_solution(3062726518476191503)
XLA Ops:
  0.0 0.7 collective-permute-start
  0.7 1.0 constant_dynamic-slice_fusion
  1.8 1.3 pad_add_fusion.meta.refs_0_
  3.1 3.3 collective-permute-done.1.theirs
  6.3 0.7 copy-done.6
  7.0 2.6 shard_map.46
  9.6 1.3 collective-permute-start.2
  10.9 8.3 %collective-permute-done.2.refs_4_ = bf16[512,256]{1,0:T(8,128)(2,1)S(1)} collective-permute-done((bf16[512,256]{1,0:T(8,128)(2,1)}, bf16[512,256]{1,0:T(8,128)(2,1)S(1)}, u32[]{:S(2)}, u32[]{:S(2)}) %collective-permute-start.2) | collective-permute-done | bytes 262176 | tf_op jit(solution)/shard_map/ppermute | solution.py:544
  19.3 1.3 collective-permute-start.3
  20.5 1.3 collective-permute-start.4
  21.8 2.2 collective-permute-start.9
  24.0 3.7 %collective-permute-done.3.refs_2_.refs_5_ = bf16[512,256]{1,0:T(8,128)(2,1)S(1)} collective-permute-done((bf16[512,256]{1,0:T(8,128)(2,1)S(1)}, bf16[512,256]{1,0:T(8,128)(2,1)S(1)}, u32[]{:S(2)}, u32[]{:S(2)}) %collective-permute-start.3) | collective-permute-done | bytes 262176 | tf_op jit(solution)/shard_map/ppermute | solution.py:544
  27.7 2.2 collective-permute-start.10
  29.9 0.7 copy-done.2
  30.6 1.3 collective-permute-start.7
  31.9 1.3 collective-permute-start.6
  33.2 1.6 collective-permute-done.9.refs_7_
  34.9 1.3 collective-permute-start.5
  36.2 1.3 collective-permute-start.8
  37.5 110.5 %shard_map.48 = (bf16[128,1536]{1,0:T(8,128)(2,1)}, bf16[128,1536]{1,0:T(8,128)(2,1)}, bf16[128,1536]{1,0:T(8,128)(2,1)}, bf16[128,1536]{1,0:T(8,128)(2,1)}) custom-call(s32[6]{0:T(128)} %pad_add_fusion.meta.refs_0_, bf16[256,6144]{1,0:T(8,128)(2,1)} %refs_1_.5, bf16[256,6144]{1,0:T(8,128)(2,1)} %collective-permute-done.refs_2_, ...), custom_call_target="tpu_custom_call" | custom-call | flops 400000000 | bytes 400000 | tf_op jit(solution)/shard_map/pallas_call | solution.py:355
  148.0 0.3 collective-permute-start.12
  148.3 6.4 %collective-permute-start.13 = (bf16[128,1536]{1,0:T(8,128)(2,1)}, bf16[128,1536]{1,0:T(8,128)(2,1)S(1)}, u32[]{:S(2)}, u32[]{:S(2)}) collective-permute-start(bf16[128,1536]{1,0:T(8,128)(2,1)} %get-tuple-element.26), channel_id=1, source_target_pairs={{0,3},{1,2},{2,1},{3,0},{4,7},{5,6},{6,5},{7,4},{8,11},{9,10},{10,... | collective-permute-start | bytes 1179656 | tf_op jit(solution)/shard_map/ppermute | solution.py:571
  154.8 0.7 copy-done.10
  155.5 14.0 %shard_map.49 = (bf16[128,1536]{1,0:T(8,128)(2,1)}, bf16[128,1536]{1,0:T(8,128)(2,1)}) custom-call(s32[6]{0:T(128)} %pad_add_fusion.meta.refs_0_, bf16[256,6144]{1,0:T(8,128)(2,1)} %refs_1_.5, bf16[256,6144]{1,0:T(8,128)(2,1)} %collective-permute-done.refs_2_, bf16[512,256]{1,0:T(8,128)(2,1)} %get-tuple-element.21.refs_3_, ...), custom_call_target="tpu_custom_call" | custom-call | flops 8000000000 | bytes 400000 | tf_op jit(solution)/shard_map/pallas_call | solution.py:355
  169.5 86.3 %collective-permute-start.16 = (bf16[128,1536]{1,0:T(8,128)(2,1)}, bf16[128,1536]{1,0:T(8,128)(2,1)S(1)}, u32[]{:S(2)}, u32[]{:S(2)}) collective-permute-start(bf16[128,1536]{1,0:T(8,128)(2,1)} %get-tuple-element.29), channel_id=1, source_target_pairs={{0,1},{1,0},{2,3},{3,2},{4,5},{5,4},{6,7},{7,6},{8,9},{9,8},{10,11... | collective-permute-start | bytes 1179656 | tf_op jit(solution)/shard_map/ppermute | solution.py:571
  255.8 0.4 collective-permute-start.15
  256.2 0.7 copy-done.7
  256.9 0.2 copy-done.8
  257.2 100.5 %shard_map.50 = (bf16[128,1536]{1,0:T(8,128)(2,1)}, bf16[128,12288]{1,0:T(8,128)(2,1)}) custom-call(s32[6]{0:T(128)} %pad_add_fusion.meta.refs_0_, bf16[256,6144]{1,0:T(8,128)(2,1)} %refs_1_.5, bf16[256,6144]{1,0:T(8,128)(2,1)} %collective-permute-done.refs_2_, bf16[512,256]{1,0:T(8,128)(2,1)} %get-tuple-element.21.refs_3_, ...), custom_call_target="tpu_custom_call" | custom-call | flops 8000000000 | bytes 400000 | tf_op jit(solution)/shard_map/pallas_call | solution.py:355
  357.7 0.4 collective-permute-start.14
  358.1 1.8 shard_map.51.refs_2_
  360.0 1.5 shard_map.52
  (38 shorter events, 0.4 us)
Async XLA Ops:
  0.0 37.5 %collective-permute-start = (bf16[256,6144]{1,0:T(8,128)(2,1)}, bf16[256,6144]{1,0:T(8,128)(2,1)}, u32[]{:S(2)}, u32[]{:S(2)}) collective-permute-start(bf16[256,6144]{1,0:T(8,128)(2,1)} %refs_1_.5), channel_id=1, source_target_pairs={{0,2},{2,0},{4,6},{6,4},{8,10},{10,8},{12,14},{14,12},{16,18},{18,... | collective-permute-start | bytes 9437192 | tf_op jit(solution)/shard_map/ppermute | solution.py:544
  1.7 4.6 %collective-permute-start.1 = (bf16[256,512]{1,0:T(8,128)(2,1)S(1)}, bf16[256,512]{1,0:T(8,128)(2,1)S(1)}, u32[]{:S(2)}, u32[]{:S(2)}) collective-permute-start(bf16[256,512]{1,0:T(8,128)(2,1)S(1)} %pad_maximum_fusion), channel_id=1, source_target_pairs={{0,2},{2,0},{4,6},{6,4},{8,10},{10,8},{12,14},{14,12},{16,18},{18,... | collective-permute-start | bytes 786440 | tf_op jit(solution)/shard_map/ppermute | solution.py:544
  6.3 0.7 copy-start.6
  9.6 9.6 %collective-permute-start.2 = (bf16[512,256]{1,0:T(8,128)(2,1)}, bf16[512,256]{1,0:T(8,128)(2,1)S(1)}, u32[]{:S(2)}, u32[]{:S(2)}) collective-permute-start(bf16[512,256]{1,0:T(8,128)(2,1)} %get-tuple-element.20.refs_3_), channel_id=1, source_target_pairs={{0,8},{2,10},{4,12},{6,14},{8,16},{10,18},{12,20},{14,22},{16,24},... | collective-permute-start | bytes 786440 | tf_op jit(solution)/shard_map/ppermute | solution.py:544
  19.3 18.2 %copy-start.3 = (bf16[512,256]{1,0:T(8,128)(2,1)}, bf16[512,256]{1,0:T(8,128)(2,1)S(1)}, u32[]{:S(2)}) copy-start(bf16[512,256]{1,0:T(8,128)(2,1)S(1)} %collective-permute-done.2.refs_4_) | copy-start | bytes 786436
  19.3 8.5 %collective-permute-start.3 = (bf16[512,256]{1,0:T(8,128)(2,1)S(1)}, bf16[512,256]{1,0:T(8,128)(2,1)S(1)}, u32[]{:S(2)}, u32[]{:S(2)}) collective-permute-start(bf16[512,256]{1,0:T(8,128)(2,1)S(1)} %collective-permute-done.2.refs_4_), channel_id=1, source_target_pairs={{0,8},{2,10},{4,12},{6,14},{8,16},{10,18},{12,20},{14,22},{16,24},... | collective-permute-start | bytes 786440 | tf_op jit(solution)/shard_map/ppermute | solution.py:544
  20.5 9.4 %collective-permute-start.4 = (bf16[512,256]{1,0:T(8,128)(2,1)}, bf16[512,256]{1,0:T(8,128)(2,1)S(1)}, u32[]{:S(2)}, u32[]{:S(2)}) collective-permute-start(bf16[512,256]{1,0:T(8,128)(2,1)} %get-tuple-element.20.refs_3_), channel_id=1, source_target_pairs={{0,4},{2,6},{8,12},{10,14},{16,20},{18,22},{24,28},{26,30},{1,5},{... | collective-permute-start | bytes 786440 | tf_op jit(solution)/shard_map/ppermute | solution.py:544
  21.8 13.0 %collective-permute-start.9 = (bf16[512,256]{1,0:T(8,128)(2,1)S(1)}, bf16[512,256]{1,0:T(8,128)(2,1)S(1)}, u32[]{:S(2)}, u32[]{:S(2)}) collective-permute-start(bf16[512,256]{1,0:T(8,128)(2,1)S(1)} %collective-permute-done.2.refs_4_), channel_id=1, source_target_pairs={{0,4},{2,6},{8,12},{10,14},{16,20},{18,22},{24,28},{26,30},{4,0},{... | collective-permute-start | bytes 786440 | tf_op jit(solution)/shard_map/ppermute | solution.py:544
  27.7 2.2 copy-start.1
  27.7 8.4 %collective-permute-start.10 = (bf16[512,256]{1,0:T(8,128)(2,1)S(1)}, bf16[512,256]{1,0:T(8,128)(2,1)S(1)}, u32[]{:S(2)}, u32[]{:S(2)}) collective-permute-start(bf16[512,256]{1,0:T(8,128)(2,1)S(1)} %collective-permute-done.3.refs_2_.refs_5_), channel_id=1, source_target_pairs={{4,0},{6,2},{12,8},{14,10},{20,16},{22,18},{28,24},{30,26},{5,1},{... | collective-permute-start | bytes 786440 | tf_op jit(solution)/shard_map/ppermute | solution.py:544
  29.9 0.7 copy-start.2
  30.6 124.1 %collective-permute-start.7 = (bf16[512,256]{1,0:T(8,128)(2,1)}, bf16[512,256]{1,0:T(8,128)(2,1)S(1)}, u32[]{:S(2)}, u32[]{:S(2)}) collective-permute-start(bf16[512,256]{1,0:T(8,128)(2,1)} %get-tuple-element.21.refs_3_), channel_id=1, source_target_pairs={{0,12},{2,14},{4,16},{6,18},{8,20},{10,22},{12,24},{14,26},{16,28}... | collective-permute-start | bytes 786440 | tf_op jit(solution)/shard_map/ppermute | solution.py:544
  31.9 122.8 %collective-permute-start.6 = (bf16[512,256]{1,0:T(8,128)(2,1)}, bf16[512,256]{1,0:T(8,128)(2,1)S(1)}, u32[]{:S(2)}, u32[]{:S(2)}) collective-permute-start(bf16[512,256]{1,0:T(8,128)(2,1)} %get-tuple-element.21.refs_3_), channel_id=1, source_target_pairs={{0,8},{2,10},{4,12},{6,14},{8,16},{10,18},{12,20},{14,22},{16,24},... | collective-permute-start | bytes 786440 | tf_op jit(solution)/shard_map/ppermute | solution.py:544
  34.9 2.6 copy-start.4
  34.9 119.9 %collective-permute-start.5 = (bf16[512,256]{1,0:T(8,128)(2,1)}, bf16[512,256]{1,0:T(8,128)(2,1)}, u32[]{:S(2)}, u32[]{:S(2)}) collective-permute-start(bf16[512,256]{1,0:T(8,128)(2,1)} %get-tuple-element.21.refs_3_), channel_id=1, source_target_pairs={{0,4},{2,6},{4,8},{6,10},{8,12},{10,14},{12,16},{14,18},{16,20},{1... | collective-permute-start | bytes 786440 | tf_op jit(solution)/shard_map/ppermute | solution.py:544
  36.2 1.3 copy-start.5
  36.2 112.2 %collective-permute-start.8 = (bf16[256,256]{1,0:T(8,128)(2,1)}, bf16[256,256]{1,0:T(8,128)(2,1)S(1)}, u32[]{:S(2)}, u32[]{:S(2)}) collective-permute-start(bf16[256,256]{1,0:T(8,128)(2,1)} %get-tuple-element.22), channel_id=1, source_target_pairs={{0,16},{2,18},{4,20},{6,22},{8,24},{10,26},{12,28},{14,30},{1,17},... | collective-permute-start | bytes 393224 | tf_op jit(solution)/shard_map/ppermute | solution.py:544
  148.0 108.1 %collective-permute-start.12 = (bf16[128,1536]{1,0:T(8,128)(2,1)}, bf16[128,1536]{1,0:T(8,128)(2,1)S(1)}, u32[]{:S(2)}, u32[]{:S(2)}) collective-permute-start(bf16[128,1536]{1,0:T(8,128)(2,1)} %get-tuple-element.25), channel_id=1, source_target_pairs={{0,1},{1,0},{2,3},{3,2},{4,5},{5,4},{6,7},{7,6},{8,9},{9,8},{10,11... | collective-permute-start | bytes 1179656 | tf_op jit(solution)/shard_map/ppermute | solution.py:571
  148.3 6.4 %copy-start.12 = (bf16[256,256]{1,0:T(8,128)(2,1)}, bf16[256,256]{1,0:T(8,128)(2,1)S(1)}, u32[]{:S(2)}) copy-start(bf16[256,256]{1,0:T(8,128)(2,1)S(1)} %collective-permute-done.8.refs_7_) | copy-start | bytes 393220
  148.3 107.8 %collective-permute-start.13 = (bf16[128,1536]{1,0:T(8,128)(2,1)}, bf16[128,1536]{1,0:T(8,128)(2,1)S(1)}, u32[]{:S(2)}, u32[]{:S(2)}) collective-permute-start(bf16[128,1536]{1,0:T(8,128)(2,1)} %get-tuple-element.26), channel_id=1, source_target_pairs={{0,3},{1,2},{2,1},{3,0},{4,7},{5,6},{6,5},{7,4},{8,11},{9,10},{10,... | collective-permute-start | bytes 1179656 | tf_op jit(solution)/shard_map/ppermute | solution.py:571
  154.7 0.7 copy-start.10
  154.7 101.5 %collective-permute-start.11 = (bf16[128,1536]{1,0:T(8,128)(2,1)}, bf16[128,1536]{1,0:T(8,128)(2,1)S(1)}, u32[]{:S(2)}, u32[]{:S(2)}) collective-permute-start(bf16[128,1536]{1,0:T(8,128)(2,1)} %get-tuple-element.24.refs_8_), channel_id=1, source_target_pairs={{0,2},{1,3},{2,0},{3,1},{4,6},{5,7},{6,4},{7,5},{8,10},{9,11},{10,... | collective-permute-start | bytes 1179656 | tf_op jit(solution)/shard_map/ppermute | solution.py:571
  154.7 0.8 copy-start.11
  169.5 188.6 %collective-permute-start.16 = (bf16[128,1536]{1,0:T(8,128)(2,1)}, bf16[128,1536]{1,0:T(8,128)(2,1)S(1)}, u32[]{:S(2)}, u32[]{:S(2)}) collective-permute-start(bf16[128,1536]{1,0:T(8,128)(2,1)} %get-tuple-element.29), channel_id=1, source_target_pairs={{0,1},{1,0},{2,3},{3,2},{4,5},{5,4},{6,7},{7,6},{8,9},{9,8},{10,11... | collective-permute-start | bytes 1179656 | tf_op jit(solution)/shard_map/ppermute | solution.py:571
  255.8 102.3 %collective-permute-start.15 = (bf16[128,1536]{1,0:T(8,128)(2,1)}, bf16[128,1536]{1,0:T(8,128)(2,1)S(1)}, u32[]{:S(2)}, u32[]{:S(2)}) collective-permute-start(bf16[128,1536]{1,0:T(8,128)(2,1)} %get-tuple-element.27.refs_12_), channel_id=1, source_target_pairs={{0,3},{1,2},{2,1},{3,0},{4,7},{5,6},{6,5},{7,4},{8,11},{9,10},{10,... | collective-permute-start | bytes 1179656 | tf_op jit(solution)/shard_map/ppermute | solution.py:571
  256.2 0.8 copy-start.7
  256.2 0.9 copy-start.8
  256.2 1.0 copy-start.9
  257.2 100.9 %copy-start = (s32[6]{0:T(128)S(1)}, s32[6]{0:T(128)}, u32[]{:S(2)}) copy-start(s32[6]{0:T(128)} %pad_add_fusion.meta.refs_0_) | copy-start | bytes 76
  357.7 2.3 collective-permute-start.14
